TPU v7x, 32 devices: a whole 2x2x4 slice. The times are simulated.
32 devices in a mesh: groups: 2 (over y), attn: 8 (over z, core), ffn: 2 (over x).
Axes of the slice: x: 2, y: 2, z: 4, core: 2. Of those that a mesh axis runs over, the one named last changes fastest.
Arguments:
- queries: bfloat16 [48, 8192], P(('groups', 'attn'), 'ffn'), parts along dimension 0, may hold values from -450 to 450
- root_keys: bfloat16 [16384, 512], P(('groups', 'attn'), 'ffn'), parts along dimension 0, may hold values from -1 to 1
- root_values: bfloat16 [16384, 512], P(('groups', 'attn'), 'ffn'), parts along dimension 0, may hold values from -6 to 6
- suffix_keys: bfloat16 [96, 128, 512], P(('groups', 'attn'), None, 'ffn'), parts along dimension 0, may hold values from -15 to 15
- suffix_values: bfloat16 [96, 128, 512], P(('groups', 'attn'), None, 'ffn'), parts along dimension 0, may hold values from -6 to 6
- suffix_lengths: int32 [48], P('groups'), parts along dimension 0, may hold values from 1 to 256, as said below
- block_table: int32 [96], P('groups'), parts along dimension 0, may hold values from 0 to 47, each once
- norm_gain: bfloat16 [8192], P('ffn'), may hold values from 0.099609375 to 1.8984375
- w_gate_up: bfloat16 [8192, 2, 26624], P('ffn', None, 'attn'), may hold values from -0.0625 to 0.0625
- w_down: bfloat16 [26624, 8192], P('attn', 'ffn'), may hold values from -0.0390625 to 0.0390625
Outputs:
- mixed: bfloat16 [48, 8192], P(('groups', 'attn'), 'ffn'), parts along dimension 0
There are 2 independent parts, one for each index of `groups`. A program takes and returns all parts, laid end to end along the dimension named above; an argument that names none is the same for every part. Nothing has to cross between parts.
Inputs may be any that keep to these rules, and one draw needn't show every extreme that they name: `suffix_lengths`: every request has at least one suffix position and some request has 256. `block_table`: each pool page is named once.
All inputs are finite; a program needn't handle non-finite values.
Results may differ from a plain program's by a relative error of at most 0.02.
Values may be sent and summed in bfloat16 or wider, within the bound.
A program may use at most 320 MiB of HBM per device.

v0:
```python
import math

import jax
import jax.numpy as jnp
from jax import lax
from jax.sharding import PartitionSpec as P

HEAD_DIM = 128
D = 8192
PAGE = 128
MAXBLK = 2


def merged(part, axis, combine):
    gathered = jax.tree.map(lambda a: lax.all_gather(a, axis), part)

    def take(source):
        return jax.tree.map(lambda a: lax.dynamic_index_in_dim(a, source, 0, False), gathered)

    return lax.fori_loop(
        1, lax.axis_size(axis), lambda source, state: combine(state, take(source)), take(0)
    )


def combine_parts(first, second):
    peak_a, total_a, summed_a = first
    peak_b, total_b, summed_b = second
    peak = jnp.maximum(peak_a, peak_b)
    factor_a = jnp.exp(peak_a - peak)
    factor_b = jnp.exp(peak_b - peak)
    return (
        peak,
        total_a * factor_a + total_b * factor_b,
        summed_a * factor_a[..., None] + summed_b * factor_b[..., None],
    )


def per_device(
    queries,
    root_keys,
    root_values,
    suffix_keys,
    suffix_values,
    suffix_lengths,
    block_table,
    norm_gain,
    w_gate_up,
    w_down,
):
    req_local = queries.shape[0]
    kv_local = root_keys.shape[1] // HEAD_DIM
    heads_local = queries.shape[1] // HEAD_DIM
    group = heads_local // kv_local
    step = math.gcd(group, 4)
    scale = HEAD_DIM ** (-0.5)
    everyone = lax.all_gather(queries, "attn", axis=0, tiled=True)
    count = everyone.shape[0]
    query_heads = everyone.reshape(count, kv_local, group, HEAD_DIM)
    blocked = query_heads.reshape(count, kv_local, group // step, step, HEAD_DIM).transpose(
        1, 2, 0, 3, 4
    )
    key_heads = root_keys.reshape(-1, kv_local, HEAD_DIM).transpose(1, 0, 2)
    value_heads = root_values.reshape(-1, kv_local, HEAD_DIM).transpose(1, 0, 2)

    def per_kv(item):
        query_kv, keys_kv, values_kv = item

        def per_block(query_block):
            scores = (
                jnp.einsum("bsd,td->bst", query_block, keys_kv, preferred_element_type=jnp.float32)
                * scale
            )
            peak = scores.max(-1)
            weights = jnp.exp(scores - peak[..., None])
            total = weights.sum(-1)
            summed = jnp.einsum(
                "bst,td->bsd",
                weights.astype(jnp.bfloat16),
                values_kv,
                preferred_element_type=jnp.float32,
            )
            return (peak, total, summed)

        return lax.map(per_block, query_kv)

    root_peak, root_total, root_summed = lax.map(per_kv, (blocked, key_heads, value_heads))
    root_peak = root_peak.transpose(2, 0, 1, 3).reshape(count, heads_local)
    root_total = root_total.transpose(2, 0, 1, 3).reshape(count, heads_local)
    root_summed = root_summed.transpose(2, 0, 1, 3, 4).reshape(count, heads_local, HEAD_DIM)
    pages_local = suffix_keys.shape[0]
    page_ids = lax.axis_index("attn") * pages_local + jnp.arange(pages_local, dtype=jnp.int32)
    slot_ids = jnp.arange(block_table.shape[0], dtype=jnp.int32)
    matches = block_table[None, :] == page_ids[:, None]
    slot = jnp.sum(jnp.where(matches, slot_ids[None, :], 0), axis=1)
    owner = slot // MAXBLK
    position = slot % MAXBLK
    valid = jnp.clip(suffix_lengths[owner] - position * PAGE, 0, PAGE)
    page_queries = query_heads[owner]
    page_keys = suffix_keys.reshape(pages_local, PAGE, kv_local, HEAD_DIM)
    page_values = suffix_values.reshape(pages_local, PAGE, kv_local, HEAD_DIM)
    alive = jnp.arange(PAGE, dtype=jnp.int32)[None, :] < valid[:, None]
    scores = (
        jnp.einsum("pkgd,ptkd->pkgt", page_queries, page_keys, preferred_element_type=jnp.float32)
        * scale
    )
    scores = jnp.where(alive[:, None, None, :], scores, -1e30)
    page_peak = scores.max(-1)
    weights = jnp.where(alive[:, None, None, :], jnp.exp(scores - page_peak[..., None]), 0.0)
    page_total = weights.sum(-1).reshape(pages_local, heads_local)
    page_summed = jnp.einsum(
        "pkgt,ptkd->pkgd",
        weights.astype(jnp.bfloat16),
        page_values,
        preferred_element_type=jnp.float32,
    )
    page_summed = page_summed.reshape(pages_local, heads_local, HEAD_DIM)
    page_peak = page_peak.reshape(pages_local, heads_local)
    belongs = owner[None, :] == jnp.arange(count, dtype=jnp.int32)[:, None]
    page_best = jnp.max(jnp.where(belongs[:, :, None], page_peak[None, :, :], -1e30), axis=1)
    peak = jnp.maximum(root_peak, page_best)
    root_factor = jnp.exp(root_peak - peak)
    page_factor = jnp.where(
        belongs[:, :, None], jnp.exp(page_peak[None, :, :] - peak[:, None, :]), 0.0
    )
    total = root_total * root_factor + jnp.sum(page_factor * page_total[None, :, :], axis=1)
    summed = root_summed * root_factor[..., None] + jnp.einsum(
        "bph,phd->bhd", page_factor, page_summed, precision=lax.Precision.HIGHEST
    )
    merged_peak, merged_total, merged_summed = merged((peak, total, summed), "attn", combine_parts)
    start = lax.axis_index("attn") * req_local
    own_total = lax.dynamic_slice_in_dim(merged_total, start, req_local, 0)
    own_summed = lax.dynamic_slice_in_dim(merged_summed, start, req_local, 0)
    attended = (own_summed / own_total[..., None]).reshape(req_local, heads_local * HEAD_DIM)
    squares = lax.psum(jnp.sum(attended * attended, axis=1), "ffn")
    hidden = (
        attended * lax.rsqrt(squares / D + 1e-05)[:, None] * norm_gain.astype(jnp.float32)[None, :]
    ).astype(jnp.bfloat16)
    units = w_gate_up.shape[2]
    joined = w_gate_up.reshape(w_gate_up.shape[0], 2 * units)
    partial_sums = jnp.dot(
        lax.all_gather(hidden, "attn", axis=0, tiled=True),
        joined,
        preferred_element_type=jnp.float32,
    )
    full_sums = lax.psum(partial_sums.astype(jnp.bfloat16), "ffn").astype(jnp.float32)
    activation = (jax.nn.silu(full_sums[:, :units]) * full_sums[:, units:]).astype(jnp.bfloat16)
    return lax.psum_scatter(
        jnp.dot(activation, w_down, preferred_element_type=jnp.float32).astype(jnp.bfloat16),
        "attn",
        scatter_dimension=0,
        tiled=True,
    )


def solution(mesh):
    return jax.shard_map(
        per_device,
        mesh=mesh,
        in_specs=(
            P(("groups", "attn"), "ffn"),
            P(("groups", "attn"), "ffn"),
            P(("groups", "attn"), "ffn"),
            P(("groups", "attn"), None, "ffn"),
            P(("groups", "attn"), None, "ffn"),
            P("groups"),
            P("groups"),
            P("ffn"),
            P("ffn", None, "attn"),
            P("attn", "ffn"),
        ),
        out_specs=P(("groups", "attn"), "ffn"),
        check_vma=False,
    )
```

profile of v0, /device:TPU:0, one launch (start us, length us, event | category | flops | bytes accessed | tf_op | source)
XLA Modules:
  0.0 259.1 jit_solution(17948314139999241645)
XLA Ops:
  6.5 16.2 %all-gather.1 = bf16[8,3,4096]{2,1,0:T(4,128)(2,1)S(1)} all-gather(bf16[1,3,4096]{2,1,0:T(4,128)(2,1)} %bitcast.174), channel_id=1, replica_groups=mesh['groups'=2,'attn'=8,'ffn'=2] {'attn'}, dimensions={0}, use_global_device_ids=true | all-gather | bytes 221184 | tf_op jit(solution)/shard_map/all_gather | solution.py:56
  23.3 0.8 select_reduce_fusion.1
  24.2 1.3 gather_fusion
  25.6 0.6 gather_fusion.1
  26.2 0.4 fusion.48
  26.7 1.3 copy.51
  28.0 1.2 copy.52
  29.3 8.5 %while.48 = (s32[]{:T(128)}, f32[2,4,24,4]{2,3,1,0:T(4,128)S(1)}, f32[2,4,24,4]{2,3,1,0:T(4,128)S(1)}, f32[2,4,24,4,128]{4,2,3,1,0:T(8,128)S(1)}, bf16[2,4,24,4,...) while((s32[]{:T(128)}, f32[2,4,24,4]{2,3,1,0:T(4,128)S(1)}, ...), condition=%wide.region_5.6_spmd, body=%wide.region_0.5_spmd.sunk | while | flops 50921280 | bytes 4705698 | solution.py:86
  29.8 3.7 %while.50 = (s32[]{:T(128)}, f32[4,24,4]{1,2,0:T(4,128)S(1)}, f32[4,24,4]{1,2,0:T(4,128)S(1)}, f32[4,24,4,128]{3,1,2,0:T(8,128)S(1)}, bf16[4,24,4,128]{3,1,2,0:T...) while((s32[]{:T(128)}, f32[4,24,4]{1,2,0:T(4,128)S(1)}, ...), condition=%wide.region_4.4_spmd, body=%wide.region_1.3_spmd.sunk | while | flops 50921280 | bytes 1789153 | solution.py:84
  29.8 0.4 fusion.66
  30.8 0.4 fusion.66
  31.7 0.4 fusion.66
  32.6 0.4 fusion.66
  34.1 3.7 %while.50 = (s32[]{:T(128)}, f32[4,24,4]{1,2,0:T(4,128)S(1)}, f32[4,24,4]{1,2,0:T(4,128)S(1)}, f32[4,24,4,128]{3,1,2,0:T(8,128)S(1)}, bf16[4,24,4,128]{3,1,2,0:T...) while((s32[]{:T(128)}, f32[4,24,4]{1,2,0:T(4,128)S(1)}, ...), condition=%wide.region_4.4_spmd, body=%wide.region_1.3_spmd.sunk | while | flops 50921280 | bytes 1789153 | solution.py:84
  34.1 0.4 fusion.66
  35.0 0.4 fusion.66
  36.0 0.4 fusion.66
  36.9 0.4 fusion.66
  37.5 0.3 fusion.68
  38.4 1.9 fusion.14
  41.0 37.6 %copy.74 = bf16[512,8,2,3328]{3,1,2,0:T(8,128)(2,1)} copy(bf16[512,8,2,3328]{3,2,1,0:T(2,128)(2,1)} %bitcast.161) | data formatting | bytes 109051904
  78.6 13.9 %all_gather.22 = f32[8,24,32]{2,1,0:T(8,128)S(1)} all-gather(f32[1,24,32]{2,1,0:T(8,128)S(1)} %copy.60), channel_id=1, replica_groups=mesh['groups'=2,'attn'=8,'ffn'=2] {'attn'}, dimensions={0}, use_global_device_ids=true | all-gather | bytes 27648 | tf_op jit(solution)/shard_map/all_gather | solution.py:15
  92.5 13.9 %all_gather.21 = f32[8,24,32]{2,1,0:T(8,128)S(1)} all-gather(f32[1,24,32]{2,1,0:T(8,128)S(1)} %copy.58), channel_id=1, replica_groups=mesh['groups'=2,'attn'=8,'ffn'=2] {'attn'}, dimensions={0}, use_global_device_ids=true | all-gather | bytes 27648 | tf_op jit(solution)/shard_map/all_gather | solution.py:15
  106.4 1.0 slice.16
  107.6 10.2 %while.49 = (s32[]{:T(128)}, f32[24,32]{1,0:T(8,128)S(1)}, f32[24,32]{1,0:T(8,128)S(1)}, f32[24,32,128]{2,1,0:T(8,128)S(1)}, f32[8,24,32]{2,1,0:T(8,128)S(1)}, /...) while((s32[]{:T(128)}, f32[24,32]{1,0:T(8,128)S(1)}, ...), condition=%wide.region_12.13_spmd, body=%wide.region_11.12_spmd.sunk | while | flops 299525 | bytes 1996951 | solution.py:20
  107.6 1.0 constant_dynamic-slice_fusion.13
  108.6 0.4 fusion.63
  109.1 1.0 constant_dynamic-slice_fusion.13
  110.1 0.4 fusion.63
  110.5 1.0 constant_dynamic-slice_fusion.13
  111.6 0.4 fusion.63
  112.0 1.0 constant_dynamic-slice_fusion.13
  113.0 0.4 fusion.63
  113.4 1.0 constant_dynamic-slice_fusion.13
  114.5 0.4 fusion.63
  114.9 1.0 constant_dynamic-slice_fusion.13
  115.9 0.4 fusion.63
  116.4 1.0 constant_dynamic-slice_fusion.13
  117.4 0.4 fusion.63
  118.0 4.9 %psum.14 = f32[3]{0:T(128)S(1)} all-reduce(f32[3]{0:T(128)S(1)} %get-tuple-element.368), channel_id=1, replica_groups=mesh['groups'=2,'attn'=8,'ffn'=2] {'ffn'}, use_global_device_ids=true, to_apply=%region_14.15 | all-reduce | flops 3 | bytes 24 | tf_op jit(solution)/shard_map/psum | solution.py:134
  123.0 14.2 %all-gather.2 = bf16[8,3,4096]{2,1,0:T(4,128)(2,1)S(1)} all-gather(bf16[1,3,4096]{2,1,0:T(4,128)(2,1)S(1)} %fusion.37), channel_id=1, replica_groups=mesh['groups'=2,'attn'=8,'ffn'=2] {'attn'}, dimensions={0}, use_global_device_ids=true | all-gather | bytes 221184 | tf_op jit(solution)/shard_map/all_gather | solution.py:141
  137.4 21.0 %convolution_convert_fusion = bf16[24,6656]{1,0:T(8,128)(2,1)} fusion(bf16[24,4096]{1,0:T(8,128)(2,1)S(1)} %reshape.282, bf16[4096,6656]{1,0:T(8,128)(2,1)} %bitcast.158), kind=kOutput, calls=%fused_computation.33 | convolution fusion | flops 1308782592 | bytes 55042048 | tf_op jit(solution)/shard_map/dot_general | solution.py:140
  158.5 25.1 %all-reduce.4.cloned.1.call-done = bf16[24,6656]{1,0:T(8,128)(2,1)} async-done(((bf16[24,6656]{1,0:T(8,128)(2,1)}), bf16[24,6656]{1,0:T(8,128)(2,1)}) %all-reduce.4.cloned.1.call-update) | async-done | bytes 319504 | tf_op jit(solution)/shard_map/psum | solution.py:145
  183.7 1.0 convert_element_type.28
  184.7 11.4 %convolution_convert_fusion.1 = bf16[24,4096]{1,0:T(8,128)(2,1)} fusion(bf16[3328,4096]{1,0:T(8,128)(2,1)} %param.25, f32[24,6656]{1,0:T(8,128)S(1)} %convert_element_type.28), kind=kOutput, calls=%fused_computation.34 | convolution fusion | flops 654888960 | bytes 28098560 | tf_op jit(solution)/shard_map/dot_general | solution.py:148
  196.2 0.6 dynamic-slice
  197.4 53.7 %all-reduce.6.cloned.1.call-done = bf16[24,4096]{1,0:T(8,128)(2,1)} async-done(((bf16[24,4096]{1,0:T(8,128)(2,1)}), bf16[24,4096]{1,0:T(8,128)(2,1)}) %all-reduce.6.cloned.1.call-update) | async-done | bytes 196624
  251.0 1.5 constant_dynamic-slice_fusion.4
  (100 shorter events, 7.7 us)
Async XLA Ops:
  6.5 19.6 %copy-start = (bf16[6,128,256]{2,1,0:T(8,128)(2,1)S(1)}, bf16[6,128,256]{2,1,0:T(8,128)(2,1)}, u32[]{:S(2)}) copy-start(bf16[6,128,256]{2,1,0:T(8,128)(2,1)} %param.19) | copy-start | bytes 1179652
  6.5 99.9 %all-gather.5.cloned.1.call-start = ((), (), s32[]{:S(2)}) async-start(), calls=%async_computation.1 | async-start | bytes 3538944 | tf_op jit(solution)/shard_map/all_gather | solution.py:15
  29.3 8.6 %copy-start.3 = (bf16[6,128,256]{2,1,0:T(8,128)(2,1)S(1)}, bf16[6,128,256]{2,1,0:T(8,128)(2,1)}, u32[]{:S(2)}) copy-start(bf16[6,128,256]{2,1,0:T(8,128)(2,1)} %param.20) | copy-start | bytes 1179652
  29.3 11.7 %copy-start.2 = (bf16[4096]{0:T(1024)(128)(2,1)S(1)}, bf16[4096]{0:T(1024)(128)(2,1)}, u32[]{:S(2)}) copy-start(bf16[4096]{0:T(1024)(128)(2,1)} %param.23) | copy-start | bytes 24580
  40.3 143.3 %all-reduce.4.cloned.1.call-start = ((), (), s32[]{:S(2)}) async-start(), calls=%async_computation | async-start | bytes 638976 | tf_op jit(solution)/shard_map/psum | solution.py:145
  137.4 115.2 %copy-start.1 = (bf16[6,128,256]{2,1,0:T(8,128)(2,1)S(1)}, bf16[6,128,256]{2,1,0:T(8,128)(2,1)}, u32[]{:S(2)}) copy-start(bf16[6,128,256]{2,1,0:T(8,128)(2,1)} %param.19) | copy-start | bytes 1179652
  158.4 37.7 %copy-start.4 = (u32[32]{0:T(128)S(1)}, u32[32]{0:T(128)}, u32[]{:S(2)}) copy-start(u32[32]{0:T(128)} %constant.155) | copy-start | bytes 388
  158.5 92.6 %all-reduce.6.cloned.1.call-start = ((), (), s32[]{:S(2)}) async-start(), calls=%async_computation.2 | async-start | bytes 393216
Sparse Core Ops, SparseCore 0:
  40.5 39.3 all-gather.4
  158.6 25.0 all-reduce.3
  196.3 54.7 all-reduce.5
where the time goes:
time: 260 us; the launch traced here: 259 us
  waiting for transfers between devices  78.8 us (30%)
  blocking collectives  63.1 us (24%)
  local copies, waits for them, and re-layouts  54.6 us (21%)
  matrix products  40.3 us (15%)
  between operations  14 us (5%)
  other arithmetic  7.45 us (3%)
    unnamed x4, waiting for transfers between devices  53.7 us
    unnamed x16, local copies, waits for them, and re-layouts  42.5 us
    all_gather x2, blocking collectives, merged(): gathered = jax.tree.map(lambda a: lax.all_gather(a, axis), part)  27.8 us
    psum x1, waiting for transfers between devices, per_device(): lax.psum(partial_sums.astype(jnp.bfloat16), 'ffn').astype(jnp.float32)  25.1 us
    dot_general x1, matrix products, per_device(): jnp.dot(lax.all_gather(hidden, 'attn', axis=0, tiled=True), joined, prefe...  21 us
    all_gather x1, blocking collectives, per_device(): everyone = lax.all_gather(queries, 'attn', axis=0, tiled=True)  16.2 us
    all_gather x1, blocking collectives, per_device(): lax.all_gather(hidden, 'attn', axis=0, tiled=True)  14.2 us
    dot_general x1, matrix products, per_device(): jnp.dot(activation, w_down, preferred_element_type=jnp.float32)  11.4 us
  transfers between devices with their start and end apart: 3, of which 2 were waited for; matrix products, arithmetic and copies ran while one was open for 15% of the time, Pallas kernels for 0%

commit v1 on v0

v1 whole, which is shorter than its diff:
```python
import functools

import jax
import jax.numpy as jnp
from jax import lax
from jax.experimental import pallas as pl
from jax.experimental.pallas import tpu as pltpu
from jax.sharding import PartitionSpec as P

HEAD_DIM = 128
PAGE = 128
MAXBLK = 2
MESH = pl.DeviceIdType.MESH


def enter(axes):
    barrier = pltpu.get_barrier_semaphore()
    greeted = 0
    for axis, size in axes:
        me = lax.axis_index(axis)
        for d in range(1, size):
            pl.semaphore_signal(
                barrier, inc=1, device_id={axis: lax.rem(me + d, size)}, device_id_type=MESH
            )
            greeted += 1
    pl.semaphore_wait(barrier, greeted)


def exchange(axis, size, source, target, sems):
    me = lax.axis_index(axis)
    copies = []
    for d in range(1, size):
        peer = lax.rem(me + d, size)
        copy = pltpu.make_async_remote_copy(
            src_ref=source(peer),
            dst_ref=target,
            send_sem=sems.at[0, d],
            recv_sem=sems.at[1, d],
            device_id={axis: peer},
            device_id_type=MESH,
        )
        copy.start()
        copies.append(copy)
    return copies


def attention_kernel(
    n, f, kv, group, q_ref, rk_ref, rv_ref, sk_ref, sv_ref, bias_ref, gain_ref, out_ref,
    qbuf, psend, precv, ssend, srecv, sqsend, sqrecv, hbuf,
    q_sems, p_sems, s_sems, sq_sems, h_sems,
):
    me = lax.axis_index("attn")
    mf = lax.axis_index("ffn")
    rows = q_ref.shape[1]
    req = rows // group
    scale = HEAD_DIM ** (-0.5)
    features = kv * group * HEAD_DIM * f
    if srecv.shape[0] > n:
        srecv[n:] = jnp.zeros_like(srecv[n:])
    enter((("attn", n), ("ffn", f)))
    sent = exchange("attn", n, lambda peer: q_ref, qbuf.at[me], q_sems)
    qbuf[me] = q_ref[...]
    for copy in sent:
        copy.wait()

    at_once = 4 if n % 4 == 0 else 1
    paged = sk_ref.shape[0]

    def block(b, carry):
        stats = []
        for k in range(kv):
            cols = slice(k * HEAD_DIM, (k + 1) * HEAD_DIM)
            query = qbuf[pl.ds(b * at_once, at_once), k].reshape(at_once * rows, HEAD_DIM)
            across = (((1,), (1,)), ((), ()))
            root = scale * lax.dot_general(
                query, rk_ref[:, cols], across, preferred_element_type=jnp.float32
            )
            page = scale * lax.dot_general(
                query, sk_ref[:, cols], across, preferred_element_type=jnp.float32
            )
            page = page.reshape(at_once * req, group, paged)
            page = page + bias_ref[pl.ds(b * at_once * req, at_once * req)]
            page = page.reshape(at_once * rows, paged)
            peak = jnp.maximum(
                jnp.max(root, axis=1, keepdims=True), jnp.max(page, axis=1, keepdims=True)
            )
            root = jnp.exp(root - peak)
            page = jnp.exp(page - peak)
            total = jnp.sum(root, axis=1, keepdims=True) + jnp.sum(page, axis=1, keepdims=True)
            summed = jnp.dot(
                root.astype(jnp.bfloat16), rv_ref[:, cols], preferred_element_type=jnp.float32
            ) + jnp.dot(
                page.astype(jnp.bfloat16), sv_ref[:, cols], preferred_element_type=jnp.float32
            )
            mean = (summed / total).astype(jnp.bfloat16)
            psend[pl.ds(b * at_once, at_once), k] = mean.reshape(at_once, rows, HEAD_DIM)
            stats.append(peak + jnp.log(total))
        lane = lax.broadcasted_iota(jnp.int32, (rows, 128), 1)
        for i in range(at_once):
            part = slice(i * rows, (i + 1) * rows)
            wide = jnp.broadcast_to(stats[0][part], (rows, 128))
            for k in range(1, kv):
                wide = jnp.where(lane % 8 >= k * (8 // kv), stats[k][part], wide)
            wide = jnp.concatenate([wide, jnp.zeros((128 - rows, 128), jnp.float32)], axis=0)
            ssend[b * at_once + i] = wide.T[:8]
        return carry

    lax.fori_loop(0, n // at_once, block, 0)

    sent = exchange("attn", n, lambda peer: ssend.at[peer], srecv.at[me], s_sems)
    sent += exchange("attn", n, lambda peer: psend.at[peer], precv.at[me], p_sems)
    srecv[me] = ssend[me]
    precv[me] = psend[me]
    for copy in sent:
        copy.wait()
    turned = [
        srecv[c * 16 : (c + 1) * 16].reshape(128, 128).T[:rows] for c in range(srecv.shape[0] // 16)
    ]
    attended = []
    for k in range(kv):
        def level(j):
            at = (j % 16) * 8 + k * (8 // kv)
            return turned[j // 16][:, at : at + 1]

        top = level(0)
        for j in range(1, n):
            top = jnp.maximum(top, level(j))
        total = jnp.zeros((rows, 1), jnp.float32)
        summed = jnp.zeros((rows, HEAD_DIM), jnp.float32)
        for j in range(n):
            weight = jnp.exp(level(j) - top)
            total = total + weight
            summed = summed + weight * precv[j, k].astype(jnp.float32)
        attended.append((summed / total).reshape(req, group, HEAD_DIM))
    squares = jnp.zeros((req, 1, 1), jnp.float32)
    for k in range(kv):
        lanes = jnp.sum(attended[k] * attended[k], axis=2, keepdims=True)
        squares = squares + jnp.sum(lanes, axis=1, keepdims=True)
    sqsend[...] = jnp.broadcast_to(squares, sqsend.shape)
    sent = exchange("ffn", f, lambda peer: sqsend, sqrecv.at[mf], sq_sems)
    sqrecv[mf] = sqsend[...]
    for copy in sent:
        copy.wait()
    whole = sqrecv[0]
    for j in range(1, f):
        whole = whole + sqrecv[j]
    factor = lax.rsqrt(whole / features + 1e-05)[:, :1, :]
    for k in range(kv):
        hidden = attended[k] * factor * gain_ref[k].astype(jnp.float32)[None]
        hbuf[me, k] = hidden.reshape(rows, HEAD_DIM).astype(jnp.bfloat16)
    sent = exchange("attn", n, lambda peer: hbuf.at[me], hbuf.at[me], h_sems)
    for copy in sent:
        copy.wait()
    out_ref[...] = hbuf[...]


def ffn_kernel(
    n, f, pieces, lhs_ref, w_ref, down_ref, out_ref,
    acc, held, xsend, xrecv, active, result, osend, orecv, d_sems, x_sems, o_sems,
):
    step = pl.program_id(0)
    me = lax.axis_index("attn")
    mf = lax.axis_index("ffn")
    chunk, _, units = w_ref.shape
    count = acc.shape[0] // 2
    req = count // n
    piece = held.shape[0] // pieces

    def fetch(i):
        at = pl.ds(pl.multiple_of(i * piece, piece), piece)
        return pltpu.make_async_copy(down_ref.at[at], held.at[at], d_sems.at[i])

    @pl.when(step == 0)
    def _():
        enter((("attn", n), ("ffn", f)))
        acc[...] = jnp.zeros_like(acc)

    @pl.when(step < pieces)
    def _():
        fetch(step).start()

    acc[...] += jnp.dot(
        lhs_ref[...], w_ref[...].reshape(2 * chunk, units), preferred_element_type=jnp.float32
    )

    @pl.when(step == pl.num_programs(0) - 1)
    def _():
        xsend[...] = acc[...].astype(jnp.bfloat16)
        sent = exchange("ffn", f, lambda peer: xsend, xrecv.at[mf], x_sems)
        for copy in sent:
            copy.wait()
        total = acc[...]
        for d in range(1, f):
            total = total + xrecv[lax.rem(mf + d, f)].astype(jnp.float32)
        gate = total[:count]
        active[...] = (gate * jax.nn.sigmoid(gate) * total[count:]).astype(jnp.bfloat16)

        def landed(i, carry):
            fetch(i).wait()
            return carry

        lax.fori_loop(0, pieces, landed, 0)
        width = result.shape[1]
        tile = 512 if width % 512 == 0 else width

        def columns(c, carry):
            at = pl.ds(pl.multiple_of(c * tile, tile), tile)
            result[:, at] = jnp.dot(
                active[...], held[:, at], preferred_element_type=jnp.float32
            )
            return carry

        lax.fori_loop(0, width // tile, columns, 0)
        for j in range(n):
            osend[j] = result[j * req : (j + 1) * req].astype(jnp.bfloat16)
        sent = exchange("attn", n, lambda peer: osend.at[peer], orecv.at[me], o_sems)
        orecv[me] = osend[me]
        for copy in sent:
            copy.wait()
        mixed = orecv[0].astype(jnp.float32)
        for j in range(1, n):
            mixed = mixed + orecv[j].astype(jnp.float32)
        out_ref[...] = mixed.astype(jnp.bfloat16)


def per_device(
    n, f, queries, root_keys, root_values, suffix_keys, suffix_values, suffix_lengths,
    block_table, norm_gain, w_gate_up, w_down,
):
    req = queries.shape[0]
    kv = root_keys.shape[1] // HEAD_DIM
    heads = queries.shape[1] // HEAD_DIM
    group = heads // kv
    rows = req * group
    count = req * n
    pages = suffix_keys.shape[0]
    width = heads * HEAD_DIM

    mine = lax.axis_index("attn") * pages + jnp.arange(pages, dtype=jnp.int32)
    offset = jnp.arange(MAXBLK, dtype=jnp.int32) * PAGE
    room = jnp.clip(suffix_lengths[:, None] - offset[None, :], 0, PAGE)
    matches = block_table.reshape(count, MAXBLK)[:, :, None] == mine[None, None, :]
    valid = jnp.sum(jnp.where(matches, room[:, :, None], 0), axis=1)
    alive = jnp.arange(PAGE, dtype=jnp.int32)[None, None, :] < valid[:, :, None]
    bias = jnp.where(alive, 0.0, -1e30).astype(jnp.float32).reshape(count, 1, pages * PAGE)

    blocked = queries.reshape(req, kv, group, HEAD_DIM).transpose(1, 0, 2, 3)
    blocked = blocked.reshape(kv, rows, HEAD_DIM)
    vmem = pl.BlockSpec(memory_space=pltpu.VMEM)
    share = (n, kv, rows, HEAD_DIM)

    def pair(size):
        return pltpu.SemaphoreType.DMA((2, size))

    hidden = pl.pallas_call(
        functools.partial(attention_kernel, n, f, kv, group),
        out_shape=jax.ShapeDtypeStruct(share, jnp.bfloat16),
        in_specs=[vmem] * 7,
        out_specs=vmem,
        scratch_shapes=[
            pltpu.VMEM(share, jnp.bfloat16),
            pltpu.VMEM(share, jnp.bfloat16),
            pltpu.VMEM(share, jnp.bfloat16),
            pltpu.VMEM((n, 8, 128), jnp.float32),
            pltpu.VMEM(((n + 15) // 16 * 16, 8, 128), jnp.float32),
            pltpu.VMEM((req, 8, 128), jnp.float32),
            pltpu.VMEM((f, req, 8, 128), jnp.float32),
            pltpu.VMEM(share, jnp.bfloat16),
            pair(n),
            pair(n),
            pair(n),
            pair(f),
            pair(n),
        ],
        compiler_params=pltpu.CompilerParams(
            collective_id=0, has_side_effects=True, vmem_limit_bytes=40 << 20
        ),
    )(
        blocked,
        root_keys,
        root_values,
        suffix_keys.reshape(pages * PAGE, kv * HEAD_DIM),
        suffix_values.reshape(pages * PAGE, kv * HEAD_DIM),
        bias,
        norm_gain.reshape(kv, group, HEAD_DIM),
    )
    hidden = hidden.reshape(n, kv, req, group, HEAD_DIM).transpose(0, 2, 1, 3, 4)
    hidden = hidden.reshape(count, width)
    blank = jnp.zeros_like(hidden)
    lhs = jnp.concatenate(
        [
            jnp.stack([hidden, blank], axis=-1).reshape(count, 2 * width),
            jnp.stack([blank, hidden], axis=-1).reshape(count, 2 * width),
        ],
        axis=0,
    )

    units = w_gate_up.shape[2]
    chunk = 128
    steps = width // chunk
    pieces = 1
    for p in range(1, steps + 1):
        if units % (16 * p) == 0:
            pieces = p
    return pl.pallas_call(
        functools.partial(ffn_kernel, n, f, pieces),
        grid=(steps,),
        out_shape=jax.ShapeDtypeStruct((req, width), jnp.bfloat16),
        in_specs=[
            pl.BlockSpec((2 * count, 2 * chunk), lambda i: (0, i)),
            pl.BlockSpec((chunk, 2, units), lambda i: (i, 0, 0)),
            pl.BlockSpec(memory_space=pl.ANY),
        ],
        out_specs=pl.BlockSpec((req, width), lambda i: (0, 0)),
        scratch_shapes=[
            pltpu.VMEM((2 * count, units), jnp.float32),
            pltpu.VMEM((units, width), jnp.bfloat16),
            pltpu.VMEM((2 * count, units), jnp.bfloat16),
            pltpu.VMEM((f, 2 * count, units), jnp.bfloat16),
            pltpu.VMEM((count, units), jnp.bfloat16),
            pltpu.VMEM((count, width), jnp.float32),
            pltpu.VMEM((n, req, width), jnp.bfloat16),
            pltpu.VMEM((n, req, width), jnp.bfloat16),
            pltpu.SemaphoreType.DMA((pieces,)),
            pair(f),
            pair(n),
        ],
        compiler_params=pltpu.CompilerParams(
            collective_id=1, has_side_effects=True, vmem_limit_bytes=52 << 20
        ),
    )(lhs, w_gate_up, w_down)


def solution(mesh):
    return jax.shard_map(
        functools.partial(per_device, mesh.shape["attn"], mesh.shape["ffn"]),
        mesh=mesh,
        in_specs=(
            P(("groups", "attn"), "ffn"),
            P(("groups", "attn"), "ffn"),
            P(("groups", "attn"), "ffn"),
            P(("groups", "attn"), None, "ffn"),
            P(("groups", "attn"), None, "ffn"),
            P("groups"),
            P("groups"),
            P("ffn"),
            P("ffn", None, "attn"),
            P("attn", "ffn"),
        ),
        out_specs=P(("groups", "attn"), "ffn"),
        check_vma=False,
    )
```

time: 260 us -> 112 us (0.43)
  Pallas kernels: 0 us -> 87.7 us
  waiting for transfers between devices: 78.8 us -> 0 us
  blocking collectives: 63.1 us -> 0 us
  matrix products: 40.3 us -> 0 us
  local copies, waits for them, and re-layouts: 54.6 us -> 22.1 us
  between operations: 14 us -> 0.11 us
  other arithmetic: 7.45 us -> 0.95 us
    pallas_call x0 -> x2, Pallas kernels: none -> 87.7 us  [the longest x1 59.2 us: per_device(): pl.pallas_call(functools.partial(ffn_kernel, n, f, pieces), grid=(steps,)...]
    all_gather x4 -> x0, blocking collectives: 58.2 us -> none  [the longest x2 27.8 us: merged(): gathered = jax.tree.map(lambda a: lax.all_gather(a, axis), part)]
    unnamed x4 -> x0, waiting for transfers between devices: 53.7 us -> none
    dot_general x21 -> x0, matrix products: 40.3 us -> none  [the longest x1 21 us: per_device(): jnp.dot(lax.all_gather(hidden, 'attn', axis=0, tiled=True), joined, prefe...]
    unnamed x16 -> x13, local copies, waits for them, and re-layouts: 42.5 us -> 9.95 us
    psum x1 -> x0, waiting for transfers between devices: 25.1 us -> none  [per_device(): lax.psum(partial_sums.astype(jnp.bfloat16), 'ffn').astype(jnp.float32)]
    dynamic_slice x21 -> x0, local copies, waits for them, and re-layouts: 9.21 us -> none  [the longest x8 8.28 us: take(): lax.dynamic_index_in_dim(a, source, 0, False)]
    another operation x1 -> x2, local copies, waits for them, and re-layouts: 0.27 us -> 8.44 us  [per_device(): jnp.stack([hidden, blank], axis=-1).reshape(count, 2 * width)]
  transfers between devices with their start and end apart: 3 -> 0, of which waited for: 2 -> 0; matrix products, arithmetic and copies ran while one was open for 15% -> 0% of each run, Pallas kernels for 0% -> 0%
where the time goes in v1:
time: 112 us; the launch traced here: 111 us
  Pallas kernels  87.7 us (78%)
  local copies, waits for them, and re-layouts  22.1 us (20%)
    pallas_call x1, Pallas kernels, per_device(): pl.pallas_call(functools.partial(ffn_kernel, n, f, pieces), grid=(steps,)...  59.2 us
    pallas_call x1, Pallas kernels, per_device(): pl.pallas_call(functools.partial(attention_kernel, n, f, kv, group), out_...  28.5 us
    unnamed x13, local copies, waits for them, and re-layouts  9.95 us
    another operation x2, local copies, waits for them, and re-layouts, per_device(): jnp.stack([hidden, blank], axis=-1).reshape(count, 2 * width)  8.44 us

profile of v1, /device:TPU:0, one launch (start us, length us, event | category | flops | bytes accessed | tf_op | source)
XLA Modules:
  0.0 110.9 jit_solution(1678042441458565381)
XLA Ops:
  0.0 0.7 subtract_clamp_fusion
  0.7 0.7 eq.15
  1.5 0.1 copy.21
  1.6 0.1 fusion
  1.7 0.1 copy.22
  1.8 0.8 copy.31
  2.5 0.1 lt.29
  2.6 0.1 lt.32
  2.7 0.1 compare_select_fusion.bias_ref
  2.8 0.0 copy-start
  2.8 1.0 copy-done
  3.8 0.0 copy-start.1
  3.8 1.0 copy-done.1
  4.9 0.0 copy-start.2
  4.9 1.0 copy-done.2
  5.9 0.0 copy-start.3
  5.9 1.0 copy-done.3
  6.8 0.0 copy-start.4
  6.8 0.7 copy-done.4
  7.5 28.5 %shard_map.100 = bf16[8,2,48,128]{3,2,1,0:T(8,128)(2,1)S(1)} custom-call(bf16[2,48,128]{2,1,0:T(8,128)(2,1)S(1)} %bitcast.22, bf16[1024,256]{1,0:T(8,128)(2,1)S(1)} %copy-done, bf16[1024,256]{1,0:T(8,128)(2,1)S(1)} %copy-done.1, bf16[768,256]{1,0:T(8,128)(2,1)S(1)} %bitcast.20, bf16[768,256]{1,0:T(8,128)(2,1)S(1)} %bitcast.21, ...), custom_call_target="tpu_custom_call" | custom-call | tf_op jit(solution)/shard_map/pallas_call | solution.py:255
  36.1 0.1 stack_reshape.4
  36.2 3.8 %copy.29 = bf16[24,4096,1]{0,2,1:T(2,128)(2,1)} copy(bf16[24,4096,1]{1,0,2:T(8,128)(2,1)S(1)} %stack_reshape.4) | data formatting | bytes 393216
  40.0 8.3 %fusion.1 = (bf16[24,4096,2]{0,2,1:T(2,128)(2,1)}, bf16[24,4096,2]{0,2,1:T(2,128)(2,1)S(1)}) fusion(bf16[24,4096,1]{0,2,1:T(2,128)(2,1)} %copy.29), kind=kLoop, calls=%fused_computation.9 | loop fusion | bytes 983040 | tf_op jit(solution)/shard_map/stack | solution.py:292
  48.4 1.8 %copy.27 = bf16[24,8192]{1,0:T(8,128)(2,1)S(1)} copy(bf16[24,8192]{0,1:T(8,128)(2,1)} %bitcast.25) | data formatting | bytes 786432 | tf_op jit(solution)/shard_map/reshape | solution.py:292
  50.2 0.8 copy.28
  51.0 0.1 pad_maximum_fusion.lhs_ref
  51.1 59.2 %shard_map.101 = bf16[3,4096]{1,0:T(4,128)(2,1)S(1)} custom-call(bf16[48,8192]{1,0:T(8,128)(2,1)S(1)} %pad_maximum_fusion.lhs_ref, bf16[4096,2,3328]{2,1,0:T(2,128)(2,1)} %w_ref.1, bf16[3328,4096]{1,0:T(8,128)(2,1)} %down_ref.1), custom_call_target="tpu_custom_call" | custom-call | tf_op jit(solution)/shard_map/pallas_call | solution.py:305
  110.2 0.6 copy.35
  (5 shorter events, 0.0 us)
Async XLA Ops:
  2.8 1.0 copy-start
  3.8 1.0 copy-start.1
  4.9 1.0 copy-start.2
  5.9 1.0 copy-start.3
  6.8 0.7 copy-start.4

commit v2 on v1

--- a/solution.py
+++ b/solution.py
@@ -151,7 +151,150 @@
     sent = exchange("attn", n, lambda peer: hbuf.at[me], hbuf.at[me], h_sems)
     for copy in sent:
         copy.wait()
-    out_ref[...] = hbuf[...]
+    if out_ref is not None:
+        out_ref[...] = hbuf[...]
+
+
+def fused_kernel(
+    n, f, kv, group, q_ref, rk_ref, rv_ref, sk_ref, sv_ref, bias_ref, gain_ref,
+    w_ref, down_ref, out_ref,
+    qbuf, psend, precv, ssend, srecv, sqsend, sqrecv, hbuf,
+    q_sems, p_sems, s_sems, sq_sems, h_sems,
+    ring, w_sems, lhs, acc, xsend, xrecv, active, result, osend, orecv, x_sems, o_sems,
+):
+    me = lax.axis_index("attn")
+    mf = lax.axis_index("ffn")
+    width, _, units = w_ref.shape
+    slots = ring.shape[0]
+    tiles = units // 128
+    steps = width // 256
+    late = steps - slots
+    count = acc.shape[0] // 2
+    req = count // n
+    pairs = w_ref.reshape(2 * width, units)
+
+    def up_load(i):
+        slot = lax.rem(i, slots)
+        at = pl.ds(pl.multiple_of(i * 512, 512), 512)
+        return [
+            pltpu.make_async_copy(
+                pairs.at[at, pl.ds(c * 128, 128)],
+                ring.at[slot, pl.ds(c * 512, 512)],
+                w_sems.at[slot, c],
+            )
+            for c in range(tiles)
+        ]
+
+    def down_load(d):
+        return [
+            pltpu.make_async_copy(
+                down_ref.at[:, pl.ds(pl.multiple_of((4 * d + t) * 128, 128), 128)],
+                ring.at[late + d, pl.ds(t * units, units)],
+                w_sems.at[late + d, t],
+            )
+            for t in range(4)
+        ]
+
+    def first(i, carry):
+        for copy in up_load(i):
+            copy.start()
+        return carry
+
+    lax.fori_loop(0, slots, first, 0)
+    attention_kernel(
+        n, f, kv, group, q_ref, rk_ref, rv_ref, sk_ref, sv_ref, bias_ref, gain_ref, None,
+        qbuf, psend, precv, ssend, srecv, sqsend, sqrecv, hbuf,
+        q_sems, p_sems, s_sems, sq_sems, h_sems,
+    )
+
+    rows = count * group
+    row = lax.broadcasted_iota(jnp.int32, (rows, rows), 0)
+    column = lax.broadcasted_iota(jnp.int32, (rows, rows), 1)
+    order = jnp.where(column == (row % count) * group + row // count, 1.0, 0.0)
+    order = order.astype(jnp.bfloat16)
+    feature = lax.broadcasted_iota(jnp.int32, (128, 256), 0)
+    spread = lax.broadcasted_iota(jnp.int32, (128, 256), 1)
+    for k in range(kv):
+        held = hbuf[:, k].reshape(rows, HEAD_DIM)
+        held = jnp.dot(order, held, preferred_element_type=jnp.float32).astype(jnp.bfloat16)
+        halves = []
+        for g in range(2):
+            place = jnp.where(spread == 2 * feature + g, 1.0, 0.0).astype(jnp.bfloat16)
+            half = jnp.dot(held, place, preferred_element_type=jnp.float32)
+            halves.append(half.reshape(group, count, 256))
+        both = jnp.concatenate(halves, axis=1).astype(jnp.bfloat16)
+        lhs[k * group : (k + 1) * group] = both
+    acc[...] = jnp.zeros_like(acc)
+
+    def multiply(i):
+        slot = lax.rem(i, slots)
+        for copy in up_load(i):
+            copy.wait()
+        left = jnp.concatenate([lhs[2 * i], lhs[2 * i + 1]], axis=1)
+        for c in range(0, tiles, 2):
+            right = jnp.concatenate(
+                [ring[slot, c * 512 : (c + 1) * 512], ring[slot, (c + 1) * 512 : (c + 2) * 512]],
+                axis=1,
+            )
+            acc[:, c * 128 : (c + 2) * 128] += jnp.dot(
+                left, right, preferred_element_type=jnp.float32
+            )
+
+    def early(i, carry):
+        multiply(i)
+        for copy in up_load(i + slots):
+            copy.start()
+        return carry
+
+    def middle(i, carry):
+        multiply(i)
+        for copy in down_load(i - late):
+            copy.start()
+        return carry
+
+    def final(i, carry):
+        multiply(i)
+        return carry
+
+    lax.fori_loop(0, late, early, 0)
+    lax.fori_loop(late, slots, middle, 0)
+    lax.fori_loop(slots, steps, final, 0)
+
+    xsend[...] = acc[...].astype(jnp.bfloat16)
+    for copy in exchange("ffn", f, lambda peer: xsend, xrecv.at[mf], x_sems):
+        copy.wait()
+    total = acc[...]
+    for d in range(1, f):
+        total = total + xrecv[lax.rem(mf + d, f)].astype(jnp.float32)
+    gate = total[:count]
+    active[...] = (gate * jax.nn.sigmoid(gate) * total[count:]).astype(jnp.bfloat16)
+
+    def columns(d, carry):
+        for copy in down_load(d):
+            copy.wait()
+        for t in range(0, 4, 2):
+            right = jnp.concatenate(
+                [
+                    ring[late + d, t * units : (t + 1) * units],
+                    ring[late + d, (t + 1) * units : (t + 2) * units],
+                ],
+                axis=1,
+            )
+            at = pl.ds(pl.multiple_of(d * 512 + t * 128, 256), 256)
+            result[:, at] = jnp.dot(active[...], right, preferred_element_type=jnp.float32)
+        return carry
+
+    lax.fori_loop(0, width // 512, columns, 0)
+    for j in range(n):
+        osend[j] = result[j * req : (j + 1) * req].astype(jnp.bfloat16)
+    sent = exchange("attn", n, lambda peer: osend.at[peer], orecv.at[me], o_sems)
+    orecv[me] = osend[me]
+    for copy in sent:
+        copy.wait()
+    mixed = orecv[0].astype(jnp.float32)
+    for j in range(1, n):
+        mixed = mixed + orecv[j].astype(jnp.float32)
+    out_ref[...] = mixed.astype(jnp.bfloat16)
 
 
 def ffn_kernel(
@@ -252,30 +395,7 @@
     def pair(size):
         return pltpu.SemaphoreType.DMA((2, size))
 
-    hidden = pl.pallas_call(
-        functools.partial(attention_kernel, n, f, kv, group),
-        out_shape=jax.ShapeDtypeStruct(share, jnp.bfloat16),
-        in_specs=[vmem] * 7,
-        out_specs=vmem,
-        scratch_shapes=[
-            pltpu.VMEM(share, jnp.bfloat16),
-            pltpu.VMEM(share, jnp.bfloat16),
-            pltpu.VMEM(share, jnp.bfloat16),
-            pltpu.VMEM((n, 8, 128), jnp.float32),
-            pltpu.VMEM(((n + 15) // 16 * 16, 8, 128), jnp.float32),
-            pltpu.VMEM((req, 8, 128), jnp.float32),
-            pltpu.VMEM((f, req, 8, 128), jnp.float32),
-            pltpu.VMEM(share, jnp.bfloat16),
-            pair(n),
-            pair(n),
-            pair(n),
-            pair(f),
-            pair(n),
-        ],
-        compiler_params=pltpu.CompilerParams(
-            collective_id=0, has_side_effects=True, vmem_limit_bytes=40 << 20
-        ),
-    )(
+    operands = (
         blocked,
         root_keys,
         root_values,
@@ -284,6 +404,58 @@
         bias,
         norm_gain.reshape(kv, group, HEAD_DIM),
     )
+    scratch = [
+        pltpu.VMEM(share, jnp.bfloat16),
+        pltpu.VMEM(share, jnp.bfloat16),
+        pltpu.VMEM(share, jnp.bfloat16),
+        pltpu.VMEM((n, 8, 128), jnp.float32),
+        pltpu.VMEM(((n + 15) // 16 * 16, 8, 128), jnp.float32),
+        pltpu.VMEM((req, 8, 128), jnp.float32),
+        pltpu.VMEM((f, req, 8, 128), jnp.float32),
+        pltpu.VMEM(share, jnp.bfloat16),
+        pair(n),
+        pair(n),
+        pair(n),
+        pair(f),
+        pair(n),
+    ]
+    units = w_gate_up.shape[2]
+    if units % 256 == 0 and width % 2048 == 0 and count % 8 == 0:
+        slots = width // 256 * 3 // 4
+        return pl.pallas_call(
+            functools.partial(fused_kernel, n, f, kv, group),
+            out_shape=jax.ShapeDtypeStruct((req, width), jnp.bfloat16),
+            in_specs=[vmem] * 7 + [pl.BlockSpec(memory_space=pl.ANY)] * 2,
+            out_specs=vmem,
+            scratch_shapes=scratch
+            + [
+                pltpu.VMEM((slots, 4 * units, 128), jnp.bfloat16),
+                pltpu.SemaphoreType.DMA((slots, units // 128)),
+                pltpu.VMEM((heads, 2 * count, 256), jnp.bfloat16),
+                pltpu.VMEM((2 * count, units), jnp.float32),
+                pltpu.VMEM((2 * count, units), jnp.bfloat16),
+                pltpu.VMEM((f, 2 * count, units), jnp.bfloat16),
+                pltpu.VMEM((count, units), jnp.bfloat16),
+                pltpu.VMEM((count, width), jnp.float32),
+                pltpu.VMEM((n, req, width), jnp.bfloat16),
+                pltpu.VMEM((n, req, width), jnp.bfloat16),
+                pair(f),
+                pair(n),
+            ],
+            compiler_params=pltpu.CompilerParams(
+                collective_id=2, has_side_effects=True, vmem_limit_bytes=58 << 20
+            ),
+        )(*operands, w_gate_up, w_down)
+    hidden = pl.pallas_call(
+        functools.partial(attention_kernel, n, f, kv, group),
+        out_shape=jax.ShapeDtypeStruct(share, jnp.bfloat16),
+        in_specs=[vmem] * 7,
+        out_specs=vmem,
+        scratch_shapes=scratch,
+        compiler_params=pltpu.CompilerParams(
+            collective_id=0, has_side_effects=True, vmem_limit_bytes=40 << 20
+        ),
+    )(*operands)
     hidden = hidden.reshape(n, kv, req, group, HEAD_DIM).transpose(0, 2, 1, 3, 4)
     hidden = hidden.reshape(count, width)
     blank = jnp.zeros_like(hidden)
@@ -295,7 +467,6 @@
         axis=0,
     )
 
-    units = w_gate_up.shape[2]
     chunk = 128
     steps = width // chunk
     pieces = 1

time: 112 us -> 73.6 us (0.66)
  Pallas kernels: 87.7 us -> 67.7 us
  local copies, waits for them, and re-layouts: 22.1 us -> 3.82 us
    pallas_call x2 -> x1, Pallas kernels: 87.7 us -> 67.7 us  [per_device(): pl.pallas_call(functools.partial(fused_kernel, n, f, kv, group), out_shap...]
    another operation x2 -> x0, local copies, waits for them, and re-layouts: 8.44 us -> none  [per_device(): jnp.stack([hidden, blank], axis=-1).reshape(count, 2 * width)]
    unnamed x13 -> x2, local copies, waits for them, and re-layouts: 9.95 us -> 2.15 us
    reshape x3 -> x0, local copies, waits for them, and re-layouts: 2.64 us -> none  [the longest x1 1.85 us: per_device(): jnp.stack([hidden, blank], axis=-1).reshape(count, 2 * width)]
where the time goes in v2:
time: 73.6 us; the launch traced here: 73.1 us
  Pallas kernels  67.7 us (92%)
  local copies, waits for them, and re-layouts  3.82 us (5%)
  other arithmetic  1.52 us (2%)
    pallas_call x1, Pallas kernels, per_device(): pl.pallas_call(functools.partial(fused_kernel, n, f, kv, group), out_shap...  67.7 us
    unnamed x2, local copies, waits for them, and re-layouts  2.15 us

profile of v2, /device:TPU:0, one launch (start us, length us, event | category | flops | bytes accessed | tf_op | source)
XLA Modules:
  0.0 73.1 jit_solution(5669187813368626931)
XLA Ops:
  0.0 0.7 %eq.15 = s32[24,2]{1,0:T(8,128)S(1)} reshape(s32[48]{0:T(128)} %param.16) | data formatting | bytes 384 | tf_op jit(solution)/shard_map/eq | solution.py:385
  0.7 0.1 copy.15
  0.8 0.7 %subtract_clamp_fusion = s32[24,2]{0,1:T(2,128)S(1)} fusion(s32[24]{0:T(128)} %param.15, s32[2]{0:T(128)S(1)} %iota_multiply_fusion), kind=kLoop, calls=%fused_computation.4 | loop fusion | flops 96 | bytes 296 | tf_op jit(solution)/shard_map/jit(clip)/min | solution.py:384
  1.6 0.1 fusion
  1.7 0.1 copy.16
  1.7 0.1 lt.29
  1.8 0.1 lt.32
  1.9 0.7 compare_select_fusion.bias_ref
  2.6 0.8 %copy.18 = bf16[1,3,32,128]{3,2,1,0:T(8,128)(2,1)S(1)} copy(bf16[1,3,32,128]{3,1,2,0:T(4,128)(2,1)} %bitcast.15) | data formatting | bytes 49152
  3.4 0.6 copy.14
  4.0 67.7 %shard_map.100 = bf16[3,4096]{1,0:T(4,128)(2,1)} custom-call(bf16[2,48,128]{2,1,0:T(8,128)(2,1)} %bitcast.13, bf16[1024,256]{1,0:T(8,128)(2,1)} %rk_ref.1, bf16[1024,256]{1,0:T(8,128)(2,1)} %rv_ref.1, bf16[768,256]{1,0:T(8,128)(2,1)} %bitcast.11, bf16[768,256]{1,0:T(8,128)(2,1)} %bitcast.12, f32[24,1,768]{2,1,0:T(1,128)} %compare_select_fusion.bias_ref, ...), custom_call_target="tpu_custom_call" | custom-call | tf_op jit(solution)/shard_map/pallas_call | solution.py:425
  71.7 1.4 %copy.20 = bf16[3,4096]{1,0:T(4,128)(2,1)} copy(bf16[3,4096]{1,0:T(4,128)(2,1)} %shard_map.100) | data formatting | bytes 49152
  (3 shorter events, 0.0 us)

commit v3 on v2

--- a/solution.py
+++ b/solution.py
@@ -47,7 +47,7 @@
 def attention_kernel(
     n, f, kv, group, q_ref, rk_ref, rv_ref, sk_ref, sv_ref, bias_ref, gain_ref, out_ref,
     qbuf, psend, precv, ssend, srecv, sqsend, sqrecv, hbuf,
-    q_sems, p_sems, s_sems, sq_sems, h_sems,
+    q_sems, p_sems, s_sems, sq_sems, h_sems, sqall=None, sqfar=None, a_sems=None,
 ):
     me = lax.axis_index("attn")
     mf = lax.axis_index("ffn")
@@ -136,6 +136,18 @@
     for k in range(kv):
         lanes = jnp.sum(attended[k] * attended[k], axis=2, keepdims=True)
         squares = squares + jnp.sum(lanes, axis=1, keepdims=True)
+    if sqall is not None:
+        for k in range(kv):
+            hidden = attended[k] * gain_ref[k].astype(jnp.float32)[None]
+            hbuf[me, k] = hidden.reshape(rows, HEAD_DIM).astype(jnp.bfloat16)
+        lines = [jnp.broadcast_to(squares[r], (1, 128)) for r in range(req)]
+        lines.append(jnp.zeros((8 - req, 128), jnp.float32))
+        sqall[me] = jnp.concatenate(lines, axis=0)
+        sent = exchange("attn", n, lambda peer: sqall.at[me], sqall.at[me], a_sems)
+        sent += exchange("attn", n, lambda peer: hbuf.at[me], hbuf.at[me], h_sems)
+        for copy in sent:
+            copy.wait()
+        return exchange("ffn", f, lambda peer: sqall, sqfar.at[mf], sq_sems)
     sqsend[...] = jnp.broadcast_to(squares, sqsend.shape)
     sent = exchange("ffn", f, lambda peer: sqsend, sqrecv.at[mf], sq_sems)
     sqrecv[mf] = sqsend[...]
@@ -161,6 +173,7 @@
     qbuf, psend, precv, ssend, srecv, sqsend, sqrecv, hbuf,
     q_sems, p_sems, s_sems, sq_sems, h_sems,
     ring, w_sems, lhs, acc, xsend, xrecv, active, result, osend, orecv, x_sems, o_sems,
+    late_sems, sqall, sqfar, a_sems,
 ):
     me = lax.axis_index("attn")
     mf = lax.axis_index("ffn")
@@ -201,10 +214,10 @@
         return carry
 
     lax.fori_loop(0, slots, first, 0)
-    attention_kernel(
+    squares_sent = attention_kernel(
         n, f, kv, group, q_ref, rk_ref, rv_ref, sk_ref, sv_ref, bias_ref, gain_ref, None,
         qbuf, psend, precv, ssend, srecv, sqsend, sqrecv, hbuf,
-        q_sems, p_sems, s_sems, sq_sems, h_sems,
+        q_sems, p_sems, s_sems, sq_sems, h_sems, sqall, sqfar, a_sems,
     )
 
     rows = count * group
@@ -266,8 +279,16 @@
     total = acc[...]
     for d in range(1, f):
         total = total + xrecv[lax.rem(mf + d, f)].astype(jnp.float32)
-    gate = total[:count]
-    active[...] = (gate * jax.nn.sigmoid(gate) * total[count:]).astype(jnp.bfloat16)
+    for copy in squares_sent:
+        copy.wait()
+    whole = sqall[...]
+    for d in range(1, f):
+        whole = whole + sqfar[lax.rem(mf + d, f)]
+    whole = jnp.concatenate([whole[j, :req] for j in range(n)], axis=0)
+    factor = lax.rsqrt(whole / (width * f) + 1e-05)[:, :1]
+    gate = total[:count] * factor
+    up = total[count:] * factor
+    active[...] = (gate * jax.nn.sigmoid(gate) * up).astype(jnp.bfloat16)
 
     def columns(d, carry):
         for copy in down_load(d):
@@ -284,17 +305,32 @@
             result[:, at] = jnp.dot(active[...], right, preferred_element_type=jnp.float32)
         return carry
 
-    lax.fori_loop(0, width // 512, columns, 0)
-    for j in range(n):
-        osend[j] = result[j * req : (j + 1) * req].astype(jnp.bfloat16)
-    sent = exchange("attn", n, lambda peer: osend.at[peer], orecv.at[me], o_sems)
-    orecv[me] = osend[me]
-    for copy in sent:
-        copy.wait()
-    mixed = orecv[0].astype(jnp.float32)
-    for j in range(1, n):
-        mixed = mixed + orecv[j].astype(jnp.float32)
-    out_ref[...] = mixed.astype(jnp.bfloat16)
+    middle_column = width // 2
+    sent = []
+    for half, sems in enumerate((o_sems, late_sems)):
+        quarter = width // 1024
+        lax.fori_loop(half * quarter, (half + 1) * quarter, columns, 0)
+        at = slice(half * middle_column, (half + 1) * middle_column)
+        for j in range(n):
+            osend[half, j] = result[j * req : (j + 1) * req, at].astype(jnp.bfloat16)
+        sent.append(
+            exchange(
+                "attn",
+                n,
+                lambda peer, half=half: osend.at[half, peer],
+                orecv.at[half, me],
+                sems,
+            )
+        )
+    for half in range(2):
+        orecv[half, me] = osend[half, me]
+        for copy in sent[half]:
+            copy.wait()
+        mixed = orecv[half, 0].astype(jnp.float32)
+        for j in range(1, n):
+            mixed = mixed + orecv[half, j].astype(jnp.float32)
+        at = slice(half * middle_column, (half + 1) * middle_column)
+        out_ref[:, at] = mixed.astype(jnp.bfloat16)
 
 
 def ffn_kernel(
@@ -420,7 +456,7 @@
         pair(n),
     ]
     units = w_gate_up.shape[2]
-    if units % 256 == 0 and width % 2048 == 0 and count % 8 == 0:
+    if units % 256 == 0 and width % 2048 == 0 and count % 8 == 0 and req < 8:
         slots = width // 256 * 3 // 4
         return pl.pallas_call(
             functools.partial(fused_kernel, n, f, kv, group),
@@ -437,9 +473,13 @@
                 pltpu.VMEM((f, 2 * count, units), jnp.bfloat16),
                 pltpu.VMEM((count, units), jnp.bfloat16),
                 pltpu.VMEM((count, width), jnp.float32),
-                pltpu.VMEM((n, req, width), jnp.bfloat16),
-                pltpu.VMEM((n, req, width), jnp.bfloat16),
+                pltpu.VMEM((2, n, req, width // 2), jnp.bfloat16),
+                pltpu.VMEM((2, n, req, width // 2), jnp.bfloat16),
                 pair(f),
+                pair(n),
+                pair(n),
+                pltpu.VMEM((n, 8, 128), jnp.float32),
+                pltpu.VMEM((f, n, 8, 128), jnp.float32),
                 pair(n),
             ],
             compiler_params=pltpu.CompilerParams(

time: 73.6 us -> 71.2 us (0.967)
  Pallas kernels: 67.7 us -> 65.5 us
    pallas_call x1, Pallas kernels: 67.7 us -> 65.5 us  [per_device(): pl.pallas_call(functools.partial(fused_kernel, n, f, kv, group), out_shap...]
where the time goes in v3:
time: 71.2 us; the launch traced here: 70.9 us
  Pallas kernels  65.5 us (92%)
  local copies, waits for them, and re-layouts  3.82 us (5%)
  other arithmetic  1.52 us (2%)
    pallas_call x1, Pallas kernels, per_device(): pl.pallas_call(functools.partial(fused_kernel, n, f, kv, group), out_shap...  65.5 us
    unnamed x2, local copies, waits for them, and re-layouts  2.15 us

profile of v3, /device:TPU:0, one launch (start us, length us, event | category | flops | bytes accessed | tf_op | source)
XLA Modules:
  0.0 70.9 jit_solution(4163308486686297974)
XLA Ops:
  0.0 0.7 %eq.15 = s32[24,2]{1,0:T(8,128)S(1)} reshape(s32[48]{0:T(128)} %param.16) | data formatting | bytes 384 | tf_op jit(solution)/shard_map/eq | solution.py:421
  0.7 0.1 copy.15
  0.8 0.7 %subtract_clamp_fusion = s32[24,2]{0,1:T(2,128)S(1)} fusion(s32[24]{0:T(128)} %param.15, s32[2]{0:T(128)S(1)} %iota_multiply_fusion), kind=kLoop, calls=%fused_computation.4 | loop fusion | flops 96 | bytes 296 | tf_op jit(solution)/shard_map/jit(clip)/min | solution.py:420
  1.6 0.1 fusion
  1.7 0.1 copy.16
  1.7 0.1 lt.29
  1.8 0.1 lt.32
  1.9 0.7 compare_select_fusion.bias_ref
  2.6 0.8 %copy.18 = bf16[1,3,32,128]{3,2,1,0:T(8,128)(2,1)S(1)} copy(bf16[1,3,32,128]{3,1,2,0:T(4,128)(2,1)} %bitcast.15) | data formatting | bytes 49152
  3.4 0.6 copy.14
  4.0 65.5 %shard_map.100 = bf16[3,4096]{1,0:T(4,128)(2,1)} custom-call(bf16[2,48,128]{2,1,0:T(8,128)(2,1)} %bitcast.13, bf16[1024,256]{1,0:T(8,128)(2,1)} %rk_ref.1, bf16[1024,256]{1,0:T(8,128)(2,1)} %rv_ref.1, bf16[768,256]{1,0:T(8,128)(2,1)} %bitcast.11, bf16[768,256]{1,0:T(8,128)(2,1)} %bitcast.12, f32[24,1,768]{2,1,0:T(1,128)} %compare_select_fusion.bias_ref, ...), custom_call_target="tpu_custom_call" | custom-call | tf_op jit(solution)/shard_map/pallas_call | solution.py:461
  69.5 1.4 %copy.20 = bf16[3,4096]{1,0:T(4,128)(2,1)} copy(bf16[3,4096]{1,0:T(4,128)(2,1)} %shard_map.100) | data formatting | bytes 49152
  (3 shorter events, 0.0 us)
